TPU v7x, 512 devices: a whole 4x4x16 slice. The times are simulated.
512 devices in a mesh: tensor: 16 (over x, z_hi), feature: 8 (over y, core), dp: 4 (over z_lo).
Axes of the slice: x: 4, y: 4, z: 16 (z_hi: 4, z_lo: 4; z = z_hi * 4 + z_lo), core: 2. Of those that a mesh axis runs over, the one named last changes fastest.
Arguments:
- mlp_input: bfloat16 [64, 4096], P(None, ('feature', 'dp')), may hold values from -6 to 6
- gate_weight: bfloat16 [4096, 28672], P(('feature', 'dp'), 'tensor'), may hold values from -0.09375 to 0.09375
- up_weight: bfloat16 [4096, 28672], P(('feature', 'dp'), 'tensor'), may hold values from -0.09375 to 0.09375
- down_weight: bfloat16 [28672, 4096], P('tensor', ('feature', 'dp')), may hold values from -0.03125 to 0.03125
- down_encoder: bfloat16 [65536, 4096], P('tensor', ('feature', 'dp')), may hold values from -6 to 6
- feature_ids: int32 [32], replicated, may hold values from 0 to 65535
- up_decoder: bfloat16 [131072, 4096], P('tensor', ('feature', 'dp')), may hold values from -0.09375 to 0.09375
- latent_ids: int32 [64, 64], replicated, may hold values from 0 to 131071, as said below
- latent_acts: float32 [64, 64], P('dp', 'tensor'), may hold values from 0.5 to 4
Outputs:
- attribution: float32 [32, 64, 64], P('feature', 'dp', 'tensor')
Inputs may be any that keep to these rules, and one draw needn't show every extreme that they name: `latent_ids`: the 64 latents of one token are distinct.
All inputs are finite; a program needn't handle non-finite values.
Results may differ from a plain program's by a relative error of at most 0.0029.
Values may be sent and summed in bfloat16 or wider, within the bound.
No kernel may reach another device: no remote copies, remote signals or barrier semaphores. Data moves between devices by JAX's collectives and lax.ppermute only.
A program may use at most 64 MiB of HBM per device.

v0:
```python
import math
import jax
import jax.numpy as jnp
from jax import lax
from jax.sharding import PartitionSpec as P


def factors(gate_pre, up_pre):
    sigmoid_gate = jax.nn.sigmoid(gate_pre)
    gate_factor = up_pre * sigmoid_gate * (1.0 + gate_pre * (1.0 - sigmoid_gate))
    up_factor = gate_pre * sigmoid_gate
    return (gate_factor, up_factor)


def arrange_blocks(partial_value, count_tensor, count_feature, count_data):
    features = partial_value.shape[0]
    tokens = partial_value.shape[1]
    slots = partial_value.shape[2]
    arranged = partial_value.reshape(
        count_feature,
        features // count_feature,
        count_data,
        tokens // count_data,
        count_tensor,
        slots // count_tensor,
    )
    arranged = arranged.transpose(4, 0, 2, 1, 3, 5)
    return arranged.reshape(
        count_tensor * count_feature * count_data,
        features // count_feature,
        tokens // count_data,
        slots // count_tensor,
    )


def on_device(
    mlp_input,
    gate_weight,
    up_weight,
    down_weight,
    down_encoder,
    feature_ids,
    up_decoder,
    latent_ids,
    latent_acts,
):
    contract = (((1,), (1,)), ((), ()))
    tensor_rank = lax.axis_index("tensor")
    tokens = mlp_input.shape[0]
    dblk = gate_weight.shape[0]
    ffblk = gate_weight.shape[1]
    features = feature_ids.shape[0]
    count_tensor = lax.axis_size("tensor")
    count_feature = lax.axis_size("feature")
    count_data = lax.axis_size("dp")
    enc_rows = down_encoder.shape[0]
    local_ids = feature_ids - tensor_rank * enc_rows
    picker = (local_ids[:, None] == jnp.arange(enc_rows, dtype=jnp.int32)[None, :]).astype(
        jnp.bfloat16
    )
    chosen = lax.psum(jnp.dot(picker, down_encoder, preferred_element_type=jnp.float32), "tensor")
    cotangent = chosen.astype(jnp.bfloat16)
    neuron_part = lax.dot_general(
        cotangent, down_weight, contract, preferred_element_type=jnp.float32
    )
    gate_part = jnp.dot(mlp_input, gate_weight, preferred_element_type=jnp.float32)
    up_part = jnp.dot(mlp_input, up_weight, preferred_element_type=jnp.float32)
    gate_pre, up_pre, neuron_grad = lax.psum((gate_part, up_part, neuron_part), ("feature", "dp"))
    gate_factor, up_factor = factors(gate_pre, up_pre)
    per_block = math.gcd(features, 8)
    grouped_rows = neuron_grad.reshape(features // per_block, per_block, ffblk)

    def feature_block(grad_rows):
        grad_gate = (
            (grad_rows[:, None, :] * gate_factor[None])
            .astype(jnp.bfloat16)
            .reshape(per_block * tokens, ffblk)
        )
        grad_up = (
            (grad_rows[:, None, :] * up_factor[None])
            .astype(jnp.bfloat16)
            .reshape(per_block * tokens, ffblk)
        )
        width_grad = lax.dot_general(
            grad_gate, gate_weight, contract, preferred_element_type=jnp.float32
        )
        width_grad = width_grad + lax.dot_general(
            grad_up, up_weight, contract, preferred_element_type=jnp.float32
        )
        return width_grad.reshape(per_block, tokens, dblk)

    width_part = lax.map(feature_block, grouped_rows).reshape(features, tokens, dblk)
    dec_rows = up_decoder.shape[0]
    local_latents = latent_ids - tensor_rank * dec_rows
    owner_mask = jnp.logical_and(local_latents >= 0, local_latents < dec_rows)
    picked = jnp.take(up_decoder, jnp.clip(local_latents, 0, dec_rows - 1), axis=0)
    picked = picked * owner_mask[:, :, None].astype(jnp.bfloat16)
    width_full = lax.psum(width_part, "tensor")
    partial_value = jnp.einsum(
        "ftd,tkd->ftk", width_full, picked.astype(jnp.float32), precision=lax.Precision.HIGHEST
    )
    arranged = arrange_blocks(partial_value, count_tensor, count_feature, count_data)
    own_block = lax.psum_scatter(
        arranged, ("tensor", "feature", "dp"), scatter_dimension=0, tiled=True
    )[0]
    return own_block * latent_acts[None, :, :]


def solution(mesh):
    in_specs = (
        P(None, ("feature", "dp")),
        P(("feature", "dp"), "tensor"),
        P(("feature", "dp"), "tensor"),
        P("tensor", ("feature", "dp")),
        P("tensor", ("feature", "dp")),
        P(),
        P("tensor", ("feature", "dp")),
        P(),
        P("dp", "tensor"),
    )
    out_specs = P("feature", "dp", "tensor")
    return jax.shard_map(
        on_device, mesh=mesh, in_specs=in_specs, out_specs=out_specs, check_vma=False
    )
```

profile of v0, /device:TPU:2, one launch (start us, length us, event | category | flops | bytes accessed | tf_op | source)
XLA Modules:
  0.0 1137.1 jit_solution(10292003025647488974)
XLA Ops:
  6.6 0.8 broadcast_subtract_fusion
  7.4 1.6 fusion.5
  9.0 99.8 %psum.35 = bf16[32,128]{1,0:T(8,128)(2,1)S(1)} all-reduce(f32[32,128]{1,0:T(8,128)S(1)} %fusion.5), channel_id=1, replica_groups=mesh['tensor'=16,'feature'=8,'dp'=4] {'tensor'}, use_global_device_ids=true, to_apply=%region_0.0 | all-reduce | flops 4096 | bytes 24576 | tf_op jit(solution)/shard_map/psum | solution.py:61
  108.8 2.0 fusion.12
  110.8 1.7 fusion.13
  112.5 1.0 convolution_bitcast_fusion
  113.5 0.0 all-reduce.10.cloned.1.call-update
  113.5 0.0 all-reduce.6.cloned.1.call-start
  113.5 283.3 %all-reduce.10.cloned.1.call-done = (f32[4,8,1792]{2,1,0:T(8,128)}, f32[64,1792]{1,0:T(8,128)}, f32[64,1792]{1,0:T(8,128)}) async-done(((f32[4,8,1792]{2,1,0:T(8,128)}, f32[64,1792]{1,0:T(8,128)}, f32[64,1792]{1,0:T(8,128)}), (f32[4,8,1792]{2,1,0:T(8,128)}, f32[64,1792]{1,0:T(8,128)}, f32[64,1792]{1,0:T(8,128)})) %all-reduce.10.cloned.1.call-update) | async-done | bytes 1146896 | tf_op jit(solution)/shard_map/psum | solution.py:68
  396.9 1.4 fusion.6
  398.2 16.5 %while.10 = (s32[]{:T(128)}, f32[4,8,64,128]{3,1,0,2:T(8,128)}, f32[4,8,1792]{2,1,0:T(8,128)}, f32[64,1792]{1,0:T(8,128)S(1)}, bf16[128,1792]{1,0:T(8,128)(2,1)S...) while((s32[]{:T(128)}, f32[4,8,64,128]{3,1,0,2:T(8,128)}, f32[4,8,1792]{2,1,0:T(8,128)}, ...), condition=%wide.region_5.6_spmd, body=%wide.region_4.5_spmd.sunk | while | flops 473497600 | bytes 12493429 | solution.py:92
  398.3 0.8 dynamic-slice_bitcast_fusion.3
  399.1 0.7 multiply_convert_fusion.3
  399.8 0.6 fusion.35
  400.5 0.4 copy-done.2
  400.8 0.6 convolution_add_fusion.2
  401.5 0.9 copy_dynamic-update-slice_fusion.2
  402.4 0.8 dynamic-slice_bitcast_fusion.3
  403.2 0.7 multiply_convert_fusion.3
  403.9 0.6 fusion.35
  404.6 0.4 copy-done.2
  404.9 0.6 convolution_add_fusion.2
  405.6 0.9 copy_dynamic-update-slice_fusion.2
  406.5 0.8 dynamic-slice_bitcast_fusion.3
  407.3 0.7 multiply_convert_fusion.3
  408.0 0.6 fusion.35
  408.7 0.4 copy-done.2
  409.0 0.6 convolution_add_fusion.2
  409.7 0.9 copy_dynamic-update-slice_fusion.2
  410.6 0.8 dynamic-slice_bitcast_fusion.3
  411.5 0.7 multiply_convert_fusion.3
  412.2 0.6 fusion.35
  412.8 0.4 copy-done.2
  413.2 0.6 convolution_add_fusion.2
  413.9 0.9 copy_dynamic-update-slice_fusion.2
  414.8 0.0 all-reduce.6.cloned.1.call-update
  414.8 0.0 all-reduce.8.cloned.1.call-start
  414.9 0.1 reshape.43
  415.0 12.1 %gather_fusion = bf16[4096,128]{1,0:T(8,128)(2,1)S(1)} fusion(bf16[8192,128]{1,0:T(8,128)(2,1)S(1)} %copy-done, s32[4096]{0:T(1024)S(1)} %broadcast_clamp_fusion), kind=kCustom, calls=%fused_computation | custom fusion | bytes 2113536 | tf_op jit(solution)/shard_map/jit(_take)/gather | solution.py:96
  427.1 197.9 %all-reduce.6.cloned.1.call-done = f32[32,64,128]{2,0,1:T(8,128)} async-done(((f32[32,64,128]{2,0,1:T(8,128)}), f32[32,64,128]{2,0,1:T(8,128)}) %all-reduce.6.cloned.1.call-update) | async-done | bytes 1048592 | tf_op jit(solution)/shard_map/psum | solution.py:98
  625.0 4.4 convolution_bitcast_fusion.1
  629.3 1.8 copy.18
  631.1 3.2 reshape.39
  634.3 3.4 copy.19
  637.7 4.7 copy.20
  642.4 0.0 all-reduce.8.cloned.1.call-update
  642.4 486.8 %all-reduce.8.cloned.1.call-done = f32[512,4,16,4]{2,3,1,0:T(4,128)} async-done(((f32[512,4,16,4]{2,3,1,0:T(4,128)}), f32[512,4,16,4]{2,3,1,0:T(4,128)}) %all-reduce.8.cloned.1.call-update) | async-done | bytes 524304
  1129.2 1.3 fusion.8
  (18 shorter events, 0.1 us)
Async XLA Ops:
  6.5 408.4 %copy-start = (bf16[8192,128]{1,0:T(8,128)(2,1)S(1)}, bf16[8192,128]{1,0:T(8,128)(2,1)}, u32[]{:S(2)}) copy-start(bf16[8192,128]{1,0:T(8,128)(2,1)} %param.17) | copy-start | bytes 6291460
  6.5 104.3 %copy-start.1 = (bf16[128,1792]{1,0:T(8,128)(2,1)S(1)}, bf16[128,1792]{1,0:T(8,128)(2,1)}, u32[]{:S(2)}) copy-start(bf16[128,1792]{1,0:T(8,128)(2,1)} %param.12) | copy-start | bytes 1376260
  6.5 106.0 %copy-start.3 = (bf16[1792,128]{1,0:T(8,128)(2,1)S(1)}, bf16[1792,128]{1,0:T(8,128)(2,1)}, u32[]{:S(2)}) copy-start(bf16[1792,128]{1,0:T(8,128)(2,1)} %param.14) | copy-start | bytes 1376260
  6.5 390.3 %all-reduce.10.cloned.1.call-start = ((), (), s32[]{:S(2)}) async-start(), calls=%async_computation.2 | async-start | bytes 2293760 | tf_op jit(solution)/shard_map/psum | solution.py:68
  113.5 511.5 %all-reduce.6.cloned.1.call-start = ((), (), s32[]{:S(2)}) async-start(), calls=%async_computation | async-start | bytes 2097152 | tf_op jit(solution)/shard_map/psum | solution.py:98
  398.2 16.6 %copy-start.4 = (s32[64,64]{1,0:T(8,128)S(1)}, s32[64,64]{1,0:T(8,128)}, u32[]{:S(2)}) copy-start(s32[64,64]{1,0:T(8,128)} %param.18) | copy-start | bytes 49156
  399.8 1.0 copy-start.2
  403.9 1.0 copy-start.2
  408.0 1.0 copy-start.2
  412.2 1.0 copy-start.2
  414.8 714.4 %all-reduce.8.cloned.1.call-start = ((), (), s32[]{:S(2)}) async-start(), calls=%async_computation.1 | async-start | bytes 8388608
  642.4 486.9 %copy-start.5 = (f32[16,4]{0,1:T(4,128)S(1)}, f32[16,4]{0,1:T(4,128)}, u32[]{:S(2)}) copy-start(f32[16,4]{0,1:T(4,128)} %param.19) | copy-start | bytes 772
Sparse Core Ops, SparseCore 0:
  113.6 283.2 all-reduce.9
  414.9 210.0 all-reduce.5
  642.5 486.6 all-reduce.7
where the time goes:
time: 1140 us
  waiting for transfers between devices  968 us (85%)
  blocking collectives  99.8 us (9%)
  local copies, waits for them, and re-layouts  33.6 us (3%)
  matrix products  15.8 us (1%)
  between operations  13.2 us (1%)
    unnamed x4, waiting for transfers between devices  487 us
    psum x1, waiting for transfers between devices, on_device(): lax.psum((gate_part, up_part, neuron_part), ('feature', 'dp'))  283 us
    psum x1, waiting for transfers between devices, on_device(): width_full = lax.psum(width_part, 'tensor')  198 us
    psum x1, blocking collectives, on_device(): lax.psum(jnp.dot(picker, down_encoder, preferred_element_type=jnp.float32...  99.8 us
  transfers between devices with their start and end apart: 3, of which 3 were waited for; matrix products, arithmetic and copies ran while one was open for 1% of the time, Pallas kernels for 0%

commit v1 on v0

--- a/solution.py
+++ b/solution.py
@@ -65,7 +65,9 @@
     )
     gate_part = jnp.dot(mlp_input, gate_weight, preferred_element_type=jnp.float32)
     up_part = jnp.dot(mlp_input, up_weight, preferred_element_type=jnp.float32)
-    gate_pre, up_pre, neuron_grad = lax.psum((gate_part, up_part, neuron_part), ("feature", "dp"))
+    gate_pre, up_pre, neuron_grad = lax.psum(
+        lax.psum((gate_part, up_part, neuron_part), "dp"), "feature"
+    )
     gate_factor, up_factor = factors(gate_pre, up_pre)
     per_block = math.gcd(features, 8)
     grouped_rows = neuron_grad.reshape(features // per_block, per_block, ffblk)

time: 1140 us -> 1010 us (0.89)
  waiting for transfers between devices: 968 us -> 839 us
    psum x1 -> x2, waiting for transfers between devices: 283 us -> 154 us  [the longest x1 80.2 us: on_device(): lax.psum(lax.psum((gate_part, up_part, neuron_part), 'dp'), 'feature')]
    unnamed x4 -> x5, waiting for transfers between devices: 487 us -> 487 us
  transfers between devices with their start and end apart: 3 -> 4, of which waited for: 3 -> 4; matrix products, arithmetic and copies ran while one was open for 1% -> 1% of each run, Pallas kernels for 0% -> 0%
where the time goes in v1:
time: 1010 us
  waiting for transfers between devices  839 us (83%)
  blocking collectives  99.8 us (10%)
  local copies, waits for them, and re-layouts  33.6 us (3%)
  matrix products  15.8 us (2%)
  between operations  13.2 us (1%)
    unnamed x5, waiting for transfers between devices  487 us
    psum x1, waiting for transfers between devices, on_device(): width_full = lax.psum(width_part, 'tensor')  199 us
    psum x1, blocking collectives, on_device(): lax.psum(jnp.dot(picker, down_encoder, preferred_element_type=jnp.float32...  99.8 us
    psum x1, waiting for transfers between devices, on_device(): lax.psum(lax.psum((gate_part, up_part, neuron_part), 'dp'), 'feature')  80.2 us
    psum x1, waiting for transfers between devices, on_device(): lax.psum((gate_part, up_part, neuron_part), 'dp')  73.8 us
  transfers between devices with their start and end apart: 4, of which 4 were waited for; matrix products, arithmetic and copies ran while one was open for 1% of the time, Pallas kernels for 0%

profile of v1, /device:TPU:2, one launch (start us, length us, event | category | flops | bytes accessed | tf_op | source)
XLA Modules:
  0.0 1008.5 jit_solution(2070131700483383995)
XLA Ops:
  6.6 0.8 broadcast_subtract_fusion
  7.4 1.6 fusion.5
  9.0 99.8 %psum.56 = bf16[32,128]{1,0:T(8,128)(2,1)S(1)} all-reduce(f32[32,128]{1,0:T(8,128)S(1)} %fusion.5), channel_id=1, replica_groups=mesh['tensor'=16,'feature'=8,'dp'=4] {'tensor'}, use_global_device_ids=true, to_apply=%region_0.0 | all-reduce | flops 4096 | bytes 24576 | tf_op jit(solution)/shard_map/psum | solution.py:61
  108.8 2.0 fusion.13
  110.8 1.7 fusion.14
  112.5 1.0 fusion.15
  113.5 0.0 all-reduce.14.cloned.1.call-update
  113.5 0.0 all-reduce.12.cloned.1.call-start
  113.5 73.8 %all-reduce.14.cloned.1.call-done = (f32[32,1792]{1,0:T(8,128)}, f32[64,1792]{1,0:T(8,128)}, f32[64,1792]{1,0:T(8,128)}) async-done(((f32[32,1792]{1,0:T(8,128)}, f32[64,1792]{1,0:T(8,128)}, f32[64,1792]{1,0:T(8,128)}), (f32[32,1792]{1,0:T(8,128)}, f32[64,1792]{1,0:T(8,128)}, f32[64,1792]{1,0:T(8,128)})) %all-reduce.14.cloned.1.call-update) | async-done | bytes 1146896 | tf_op jit(solution)/shard_map/psum | solution.py:69
  187.4 0.0 all-reduce.8.cloned.1.call-start
  187.5 80.2 %all-reduce.12.cloned.1.call-done = (f32[4,8,1792]{2,1,0:T(8,128)}, f32[64,1792]{1,0:T(8,128)}, f32[64,1792]{1,0:T(8,128)}) async-done(((f32[4,8,1792]{2,1,0:T(8,128)}, f32[64,1792]{1,0:T(8,128)}, f32[64,1792]{1,0:T(8,128)}), (f32[4,8,1792]{2,1,0:T(8,128)}, f32[64,1792]{1,0:T(8,128)}, f32[64,1792]{1,0:T(8,128)})) %all-reduce.12.cloned.1.call-update) | async-done | bytes 1146896 | tf_op jit(solution)/shard_map/psum | solution.py:68
  267.7 1.4 fusion.6
  269.1 16.5 %while.10 = (s32[]{:T(128)}, f32[4,8,64,128]{3,1,0,2:T(8,128)}, f32[4,8,1792]{2,1,0:T(8,128)}, f32[64,1792]{1,0:T(8,128)S(1)}, bf16[128,1792]{1,0:T(8,128)(2,1)S...) while((s32[]{:T(128)}, f32[4,8,64,128]{3,1,0,2:T(8,128)}, f32[4,8,1792]{2,1,0:T(8,128)}, ...), condition=%wide.region_8.9_spmd, body=%wide.region_7.8_spmd.sunk | while | flops 473497600 | bytes 12493429 | solution.py:94
  269.1 0.8 dynamic-slice_bitcast_fusion.3
  269.9 0.7 multiply_convert_fusion.3
  270.6 0.6 fusion.37
  271.3 0.4 copy-done.2
  271.7 0.6 convolution_add_fusion.2
  272.3 0.9 copy_dynamic-update-slice_fusion.2
  273.2 0.8 dynamic-slice_bitcast_fusion.3
  274.0 0.7 multiply_convert_fusion.3
  274.7 0.6 fusion.37
  275.4 0.4 copy-done.2
  275.8 0.6 convolution_add_fusion.2
  276.4 0.9 copy_dynamic-update-slice_fusion.2
  277.3 0.8 dynamic-slice_bitcast_fusion.3
  278.1 0.7 multiply_convert_fusion.3
  278.9 0.6 fusion.37
  279.5 0.4 copy-done.2
  279.9 0.6 convolution_add_fusion.2
  280.5 0.9 copy_dynamic-update-slice_fusion.2
  281.4 0.8 dynamic-slice_bitcast_fusion.3
  282.3 0.7 multiply_convert_fusion.3
  283.0 0.6 fusion.37
  283.7 0.4 copy-done.2
  284.0 0.6 convolution_add_fusion.2
  284.7 0.9 copy_dynamic-update-slice_fusion.2
  285.6 0.0 all-reduce.10.cloned.1.call-start
  285.7 0.1 reshape.43
  285.8 12.1 %gather_fusion = bf16[4096,128]{1,0:T(8,128)(2,1)S(1)} fusion(bf16[8192,128]{1,0:T(8,128)(2,1)S(1)} %copy-done, s32[4096]{0:T(1024)S(1)} %broadcast_clamp_fusion), kind=kCustom, calls=%fused_computation | custom fusion | bytes 2113536 | tf_op jit(solution)/shard_map/jit(_take)/gather | solution.py:98
  297.9 198.5 %all-reduce.8.cloned.1.call-done = f32[32,64,128]{2,0,1:T(8,128)} async-done(((f32[32,64,128]{2,0,1:T(8,128)}), f32[32,64,128]{2,0,1:T(8,128)}) %all-reduce.8.cloned.1.call-update) | async-done | bytes 1048592 | tf_op jit(solution)/shard_map/psum | solution.py:100
  496.4 4.4 convolution_bitcast_fusion
  500.8 1.8 copy.18
  502.6 3.2 reshape.39
  505.8 3.4 copy.19
  509.1 4.7 copy.20
  513.8 486.8 %all-reduce.10.cloned.1.call-done = f32[512,4,16,4]{2,3,1,0:T(4,128)} async-done(((f32[512,4,16,4]{2,3,1,0:T(4,128)}), f32[512,4,16,4]{2,3,1,0:T(4,128)}) %all-reduce.10.cloned.1.call-update) | async-done | bytes 524304
  1000.7 1.3 fusion.8
  (21 shorter events, 0.1 us)
Async XLA Ops:
  6.5 279.2 %copy-start = (bf16[8192,128]{1,0:T(8,128)(2,1)S(1)}, bf16[8192,128]{1,0:T(8,128)(2,1)}, u32[]{:S(2)}) copy-start(bf16[8192,128]{1,0:T(8,128)(2,1)} %param.17) | copy-start | bytes 6291460
  6.5 104.3 %copy-start.1 = (bf16[128,1792]{1,0:T(8,128)(2,1)S(1)}, bf16[128,1792]{1,0:T(8,128)(2,1)}, u32[]{:S(2)}) copy-start(bf16[128,1792]{1,0:T(8,128)(2,1)} %param.12) | copy-start | bytes 1376260
  6.5 105.9 %copy-start.3 = (bf16[1792,128]{1,0:T(8,128)(2,1)S(1)}, bf16[1792,128]{1,0:T(8,128)(2,1)}, u32[]{:S(2)}) copy-start(bf16[1792,128]{1,0:T(8,128)(2,1)} %param.14) | copy-start | bytes 1376260
  6.5 180.8 %all-reduce.14.cloned.1.call-start = ((), (), s32[]{:S(2)}) async-start(), calls=%async_computation.3 | async-start | bytes 2293760 | tf_op jit(solution)/shard_map/psum | solution.py:69
  113.5 154.2 %all-reduce.12.cloned.1.call-start = ((), (), s32[]{:S(2)}) async-start(), calls=%async_computation.2 | async-start | bytes 2293760 | tf_op jit(solution)/shard_map/psum | solution.py:68
  187.4 309.0 %all-reduce.8.cloned.1.call-start = ((), (), s32[]{:S(2)}) async-start(), calls=%async_computation | async-start | bytes 2097152 | tf_op jit(solution)/shard_map/psum | solution.py:100
  269.0 16.6 %copy-start.4 = (s32[64,64]{1,0:T(8,128)S(1)}, s32[64,64]{1,0:T(8,128)}, u32[]{:S(2)}) copy-start(s32[64,64]{1,0:T(8,128)} %param.18) | copy-start | bytes 49156
  270.6 1.0 copy-start.2
  274.7 1.0 copy-start.2
  278.8 1.0 copy-start.2
  283.0 1.0 copy-start.2
  285.6 715.1 %all-reduce.10.cloned.1.call-start = ((), (), s32[]{:S(2)}) async-start(), calls=%async_computation.1 | async-start | bytes 8388608
  513.8 486.8 %copy-start.5 = (f32[16,4]{0,1:T(4,128)S(1)}, f32[16,4]{0,1:T(4,128)}, u32[]{:S(2)}) copy-start(f32[16,4]{0,1:T(4,128)} %param.19) | copy-start | bytes 772
Sparse Core Ops, SparseCore 0:
  113.6 73.7 all-reduce.13
  189.9 77.6 all-reduce.11
  285.7 210.6 all-reduce.7
  514.0 486.6 all-reduce.9
